TPU v7x, 512 devices: a whole 4x4x16 slice. The times are simulated.
512 devices in a mesh: rep: 16 (over z), ep: 32 (over y, x, core).
Axes of the slice: x: 4, y: 4, z: 16, core: 2. Of those that a mesh axis runs over, the one named last changes fastest.
Arguments:
- tokens: bfloat16 [2048, 4096], P('rep'), may hold values from -6 to 6
- routes: int32 [2048, 2], P('rep'), may hold values from 0 to 7, all different within a row; in each aligned block of 128 rows (0 to 127, 128 to 255, ...) at most 64 rows name the same one
- gates: bfloat16 [2048, 2], P('rep'), may hold values from 0.19921875 to 1
- w_gate: bfloat16 [32, 1792, 4096], P('ep', 'rep'), may hold values from -0.09375 to 0.09375
- w_up: bfloat16 [32, 1792, 4096], P('ep', 'rep'), may hold values from -0.09375 to 0.09375
- direction: bfloat16 [32, 1792, 4096], P('ep', None, 'rep'), may hold values from -32 to 32
Outputs:
- next_direction: bfloat16 [32, 1792, 4096], P('ep', None, 'rep')
- rayleigh: float32 [1], replicated
Inputs may be any that keep to these rules, and one draw needn't show every extreme that they name: `routes`: each row names two different experts. In each aligned block of 128 rows (the tokens of one replica) no expert is named by more than 64 rows, and in some block some expert is named by exactly 64 rows.
All inputs are finite; a program needn't handle non-finite values.
Results may differ from a plain program's by a relative error of at most 0.007.
Values may be sent and summed in bfloat16 or wider, within the bound.
A program may use at most 64 MiB of HBM per device.

v0:
```python
import jax
import jax.numpy as jnp
from jax import lax
from jax.sharding import PartitionSpec as P

D = 4096
FF = 7168
EXPERTS = 8
ITERS = 2
CAP = 64


def own_slots(route_rows, expert, depth):
    pairs = route_rows.reshape(-1)
    hits = (pairs == expert).astype(jnp.int32)
    rank = jnp.cumsum(hits) - hits
    slots = jnp.arange(depth, dtype=jnp.int32)[:, None]
    return ((slots == rank[None, :]) & (hits[None, :] > 0)).astype(jnp.float32)


def on_device(tokens, routes, gates, w_gate, w_up, direction):
    n_rep = lax.axis_size("rep")
    n_ep = lax.axis_size("ep")
    slices = n_ep // EXPERTS
    local = tokens.shape[0]
    depth = CAP
    expert = lax.axis_index("ep") // slices
    route_all = lax.all_gather(routes, "rep", axis=0, tiled=True).reshape(n_rep, local, 2)
    tables = jax.vmap(lambda chosen: own_slots(chosen, expert, depth))(route_all)
    token_map = tables.reshape(n_rep, depth, local, 2).sum(axis=3)
    own_table = lax.dynamic_index_in_dim(tables, lax.axis_index("rep"), 0, keepdims=False)
    own_tokens = own_table.reshape(depth, local, 2).sum(axis=2)
    picked = jnp.dot(
        own_tokens.astype(jnp.bfloat16), tokens, preferred_element_type=jnp.float32
    ).astype(jnp.bfloat16)
    picked_gate = jnp.dot(
        own_table, gates.reshape(-1).astype(jnp.float32), precision=lax.Precision.HIGHEST
    ).astype(jnp.bfloat16)
    rows, rates = (
        lax.all_gather(picked, "rep", axis=0, tiled=True),
        lax.all_gather(picked_gate, "rep", axis=0, tiled=True),
    )
    contract = (((1,), (1,)), ((), ()))
    pre_gate = lax.dot_general(w_gate[0], rows, contract, preferred_element_type=jnp.float32)
    pre_up = lax.dot_general(w_up[0], rows, contract, preferred_element_type=jnp.float32)
    gated = (jax.nn.silu(pre_gate) * pre_up * rates.astype(jnp.float32)[None, :]).astype(
        jnp.bfloat16
    )
    hidden_t = lax.all_gather(gated, "rep", axis=0, tiled=True)
    current = direction[0]
    columns = current.shape[1]
    count = float(EXPERTS * FF * D)
    rayleigh = jnp.zeros((), jnp.float32)
    first_dims = (((0,), (0,)), ((), ()))
    for step in range(ITERS):
        partial_value = lax.dot_general(
            hidden_t, current, first_dims, preferred_element_type=jnp.float32
        ).reshape(n_rep, depth, columns)
        spread = jnp.einsum(
            "rst,rsd->rtd", token_map, partial_value, precision=lax.Precision.HIGHEST
        ).reshape(n_rep * local, columns)
        tangent = lax.psum_scatter(spread, "ep", scatter_dimension=0, tiled=True)
        piece = tangent.astype(jnp.bfloat16)
        sent = lax.all_gather(piece, "ep", axis=0, tiled=True)
        current_f = current.astype(jnp.float32)
        arrived = jnp.einsum(
            "rst,rtd->rsd",
            token_map.astype(jnp.bfloat16),
            sent.reshape(n_rep, local, columns),
            preferred_element_type=jnp.float32,
        ).astype(jnp.bfloat16)
        product = (
            jnp.dot(
                hidden_t,
                arrived.reshape(n_rep * depth, columns),
                preferred_element_type=jnp.float32,
            )
            / n_rep
        )
        energy, cross, square = lax.psum(
            (
                jnp.sum(product * product),
                jnp.sum(current_f * product),
                jnp.sum(current_f * current_f),
            ),
            ("rep", "ep"),
        )
        rayleigh = cross / count / (square / count + 1e-06)
        current = (product * lax.rsqrt(energy / count + 1e-06)).astype(jnp.bfloat16)
    return (current[None], rayleigh.reshape(1))


def solution(mesh):
    return jax.shard_map(
        on_device,
        mesh=mesh,
        in_specs=(
            P("rep", None),
            P("rep", None),
            P("rep", None),
            P("ep", "rep", None),
            P("ep", "rep", None),
            P("ep", None, "rep"),
        ),
        out_specs=(P("ep", None, "rep"), P()),
        check_vma=False,
    )
```

profile of v0, /device:TPU:1, one launch (start us, length us, event | category | flops | bytes accessed | tf_op | source)
XLA Modules:
  0.0 805.5 jit_solution(234640360543273105)
XLA Ops:
  7.2 29.7 %all_gather.18 = s32[2048,2]{0,1:T(2,128)S(1)} all-gather(s32[128,2]{0,1:T(2,128)} %param.7), channel_id=1, replica_groups=mesh['rep'=16,'ep'=32] {'rep'}, dimensions={0}, use_global_device_ids=true | all-gather | bytes 17408 | tf_op jit(solution)/shard_map/all_gather | solution.py:28
  37.0 0.4 copy.50
  37.3 0.6 reshape.108
  38.0 0.5 reshape.109
  38.4 0.6 reduce-window.6
  39.3 1.4 fusion
  41.0 1.1 convolution_convert_fusion
  42.5 1.3 dynamic-slice
  44.7 20.1 %all-reduce = bf16[1024]{0:T(1024)(128)(2,1)S(1)} all-reduce(bf16[1024]{0:T(1024)(128)(2,1)S(1)} %dynamic-update-slice), channel_id=1, replica_groups=mesh['rep'=16,'ep'=32] {'rep'}, use_global_device_ids=true, to_apply=%add | all-reduce | flops 1024 | bytes 4096
  64.8 86.5 %all-gather.5.cloned.1.call-done = bf16[1024,4096]{1,0:T(8,128)(2,1)} async-done(((bf16[64,4096]{1,0:T(8,128)(2,1)}), bf16[1024,4096]{1,0:T(8,128)(2,1)}) %all-gather.5.cloned.1.call-update) | async-done | bytes 8388624 | tf_op jit(solution)/shard_map/all_gather | solution.py:40
  151.3 6.4 convolution_bitcast_fusion.1
  157.7 3.5 fusion.5
  161.8 0.2 convert_reduce_fusion
  162.1 66.3 %all-gather.7.cloned.1.call-done = bf16[1792,1024]{1,0:T(8,128)(2,1)} async-done(((bf16[112,1024]{1,0:T(8,128)(2,1)}), bf16[1792,1024]{1,0:T(8,128)(2,1)}) %all-gather.7.cloned.1.call-update) | async-done | bytes 3670032 | tf_op jit(solution)/shard_map/all_gather | solution.py:49
  228.3 6.0 copy.60
  234.4 3.2 fusion.9
  237.5 3.2 fusion.20
  240.8 105.8 %reduce-scatter.3.cloned.1.call-done = f32[64,256]{1,0:T(8,128)} async-done(((f32[2048,256]{1,0:T(8,128)}), f32[64,256]{1,0:T(8,128)}) %reduce-scatter.3.cloned.1.call-update) | async-done | bytes 65552 | tf_op jit(solution)/shard_map/reduce_scatter | solution.py:62
  346.6 1.5 convert_element_type.87
  348.3 61.5 %all-gather.9.cloned.1.call-done = bf16[2048,256]{1,0:T(8,128)(2,1)} async-done(((bf16[64,256]{1,0:T(8,128)(2,1)}), bf16[2048,256]{1,0:T(8,128)(2,1)}) %all-gather.9.cloned.1.call-update) | async-done | bytes 1048592 | tf_op jit(solution)/shard_map/all_gather | solution.py:64
  409.8 1.5 convolution_convert_fusion.2
  411.3 3.8 multiply_reduce_fusion.1
  415.1 103.6 %psum.28 = f32[]{:T(128)} all-reduce(f32[]{:T(128)} %get-tuple-element.8), channel_id=1, replica_groups=mesh['rep'=16,'ep'=32] {'rep','ep'}, use_global_device_ids=true, to_apply=%region_6.7 | all-reduce | flops 1 | bytes 8 | tf_op jit(solution)/shard_map/psum | solution.py:80
  519.4 3.2 fusion.19
  522.6 3.2 fusion.21
  526.0 95.4 %reduce-scatter.5.cloned.1.call-done = f32[64,256]{1,0:T(8,128)} async-done(((f32[2048,256]{1,0:T(8,128)}), f32[64,256]{1,0:T(8,128)}) %reduce-scatter.5.cloned.1.call-update) | async-done | bytes 65552 | tf_op jit(solution)/shard_map/reduce_scatter | solution.py:62
  621.3 1.5 convert_element_type.90
  622.8 61.7 %all-gather.11.cloned.1.call-done = bf16[2048,256]{1,0:T(8,128)(2,1)} async-done(((bf16[64,256]{1,0:T(8,128)(2,1)}), bf16[2048,256]{1,0:T(8,128)(2,1)}) %all-gather.11.cloned.1.call-update) | async-done | bytes 1048592 | tf_op jit(solution)/shard_map/all_gather | solution.py:64
  684.5 1.5 convolution_convert_fusion.1
  686.1 4.6 fusion.1
  690.6 103.8 %all-reduce.1 = (f32[]{:T(128)}, f32[]{:T(128)}, f32[]{:T(128)}) all-reduce(f32[]{:T(128)} %get-tuple-element.3, f32[]{:T(128)} %get-tuple-element.2, f32[]{:T(128)} %get-tuple-element.4), channel_id=1, replica_groups=mesh['rep'=16,'ep'=32] {'rep','ep'}, use_global_device_ids=true, to_apply=%region_9.10 | all-reduce | flops 3 | bytes 24 | tf_op jit(solution)/shard_map/psum | solution.py:80
  796.5 1.1 fusion.8
  (51 shorter events, 2.1 us)
Async XLA Ops:
  7.2 33.8 %copy-start = (bf16[128,4096]{1,0:T(8,128)(2,1)S(1)}, bf16[128,4096]{1,0:T(8,128)(2,1)}, u32[]{:S(2)}) copy-start(bf16[128,4096]{1,0:T(8,128)(2,1)} %param.6) | copy-start | bytes 3145732
  7.2 144.1 %all-gather.5.cloned.1.call-start = ((), (), s32[]{:S(2)}) async-start(), calls=%async_computation.2 | async-start | bytes 8912896 | tf_op jit(solution)/shard_map/all_gather | solution.py:40
  37.9 4.2 copy-start.1
  38.0 113.3 %copy-start.3 = (bf16[1,112,4096]{2,1,0:T(8,128)(2,1)S(1)}, bf16[1,112,4096]{2,1,0:T(8,128)(2,1)}, u32[]{:S(2)}) copy-start(bf16[1,112,4096]{2,1,0:T(8,128)(2,1)} %param.9) | copy-start | bytes 2752516
  42.1 186.2 %all-gather.7.cloned.1.call-start = ((), (), s32[]{:S(2)}) async-start(), calls=%async_computation.3 | async-start | bytes 3899392 | tf_op jit(solution)/shard_map/all_gather | solution.py:49
  151.3 6.4 copy-start.2
  151.3 6.4 copy-start.4
  161.3 185.3 %reduce-scatter.3.cloned.1.call-start = ((), (), s32[]{:S(2)}) async-start(), calls=%async_computation.4 | async-start | bytes 2162688 | tf_op jit(solution)/shard_map/reduce_scatter | solution.py:62
  228.3 6.0 copy-start.5
  240.8 169.0 %all-gather.9.cloned.1.call-start = ((), (), s32[]{:S(2)}) async-start(), calls=%async_computation.5 | async-start | bytes 1081344 | tf_op jit(solution)/shard_map/all_gather | solution.py:64
  348.1 273.2 %reduce-scatter.5.cloned.1.call-start = ((), (), s32[]{:S(2)}) async-start(), calls=%async_computation.6 | async-start | bytes 2162688 | tf_op jit(solution)/shard_map/reduce_scatter | solution.py:62
  415.1 107.5 %copy-start.6 = (f32[1792,256]{1,0:T(8,128)}, f32[1792,256]{1,0:T(8,128)S(1)}, u32[]{:S(2)}) copy-start(f32[1792,256]{1,0:T(8,128)S(1)} %get-tuple-element.9) | copy-start | bytes 5505028
  525.9 158.6 %all-gather.11.cloned.1.call-start = ((), (), s32[]{:S(2)}) async-start(), calls=%async_computation.7 | async-start | bytes 1081344 | tf_op jit(solution)/shard_map/all_gather | solution.py:64
Sparse Core Ops, SparseCore 0:
  42.2 109.0 all-gather.4
  161.4 66.8 all-gather.6
  240.9 105.6 reduce-scatter.2
  350.2 59.5 all-gather.8
  526.0 95.2 reduce-scatter.4
  624.9 59.5 all-gather.10
where the time goes:
time: 806 us
  waiting for transfers between devices  477 us (59%)
  blocking collectives  257 us (32%)
  matrix products  35.4 us (4%)
  between operations  18.9 us (2%)
  local copies, waits for them, and re-layouts  9.84 us (1%)
    psum x2, blocking collectives, on_device(): lax.psum((jnp.sum(product * product), jnp.sum(current_f * product), jnp.s...  207 us
    reduce_scatter x2, waiting for transfers between devices, on_device(): tangent = lax.psum_scatter(spread, 'ep', scatter_dimension=0, tiled=True)  201 us
    all_gather x2, waiting for transfers between devices, on_device(): sent = lax.all_gather(piece, 'ep', axis=0, tiled=True)  123 us
    all_gather x1, waiting for transfers between devices, on_device(): lax.all_gather(picked, 'rep', axis=0, tiled=True)  86.5 us
    all_gather x1, waiting for transfers between devices, on_device(): hidden_t = lax.all_gather(gated, 'rep', axis=0, tiled=True)  66.3 us
    all_gather x1, blocking collectives, on_device(): lax.all_gather(routes, 'rep', axis=0, tiled=True).reshape(n_rep, local, 2)  29.7 us
    unnamed x1, blocking collectives  20.1 us
  transfers between devices with their start and end apart: 6, of which 6 were waited for; matrix products, arithmetic and copies ran while one was open for 0% of the time, Pallas kernels for 0%

commit v1 on v0

--- a/solution.py
+++ b/solution.py
@@ -8,6 +8,18 @@
 EXPERTS = 8
 ITERS = 2
 CAP = 64
+
+
+def gather_by_bits(x, axis, dim):
+    ways, here = (lax.axis_size(axis), lax.axis_index(axis))
+    grown, reach = (x, 1)
+    while reach < ways:
+        theirs = lax.ppermute(grown, axis, [(d, d ^ reach) for d in range(ways)])
+        mine_first = jnp.concatenate([grown, theirs], axis=dim)
+        theirs_first = jnp.concatenate([theirs, grown], axis=dim)
+        grown = jnp.where(here & reach == 0, mine_first, theirs_first)
+        reach = 2 * reach
+    return grown
 
 
 def own_slots(route_rows, expert, depth):
@@ -37,7 +49,7 @@
         own_table, gates.reshape(-1).astype(jnp.float32), precision=lax.Precision.HIGHEST
     ).astype(jnp.bfloat16)
     rows, rates = (
-        lax.all_gather(picked, "rep", axis=0, tiled=True),
+        gather_by_bits(picked, "rep", 0),
         lax.all_gather(picked_gate, "rep", axis=0, tiled=True),
     )
     contract = (((1,), (1,)), ((), ()))

time: 806 us -> 1330 us (1.65)
  blocking collectives: 257 us -> 510 us
  waiting for transfers between devices: 477 us -> 721 us
  starting transfers between devices: 0.43 us -> 13.9 us
    ppermute x0 -> x4, waiting for transfers between devices: none -> 326 us  [gather_by_bits(): theirs = lax.ppermute(grown, axis, [(d, d ^ reach) for d in range(ways)])]
    unnamed x1, blocking collectives: 20.1 us -> 273 us
    all_gather x1 -> x0, waiting for transfers between devices: 86.5 us -> none  [on_device(): lax.all_gather(picked, 'rep', axis=0, tiled=True)]
    ppermute x0 -> x4, starting transfers between devices: none -> 13.6 us  [gather_by_bits(): theirs = lax.ppermute(grown, axis, [(d, d ^ reach) for d in range(ways)])]
  transfers between devices with their start and end apart: 6 -> 9, of which waited for: 6 -> 8; matrix products, arithmetic and copies ran while one was open for 0% -> 0% of each run, Pallas kernels for 0% -> 0%
where the time goes in v1:
time: 1330 us
  waiting for transfers between devices  721 us (54%)
  blocking collectives  510 us (38%)
  matrix products  41.3 us (3%)
  between operations  18.6 us (1%)
  other arithmetic  14.5 us (1%)
  starting transfers between devices  13.9 us (1%)
    ppermute x4, waiting for transfers between devices, gather_by_bits(): theirs = lax.ppermute(grown, axis, [(d, d ^ reach) for d in range(ways)])  326 us
    unnamed x1, blocking collectives  273 us
    psum x2, blocking collectives, on_device(): lax.psum((jnp.sum(product * product), jnp.sum(current_f * product), jnp.s...  207 us
    reduce_scatter x2, waiting for transfers between devices, on_device(): tangent = lax.psum_scatter(spread, 'ep', scatter_dimension=0, tiled=True)  201 us
    all_gather x2, waiting for transfers between devices, on_device(): sent = lax.all_gather(piece, 'ep', axis=0, tiled=True)  123 us
    all_gather x1, waiting for transfers between devices, on_device(): hidden_t = lax.all_gather(gated, 'rep', axis=0, tiled=True)  70.2 us
    all_gather x1, blocking collectives, on_device(): lax.all_gather(routes, 'rep', axis=0, tiled=True).reshape(n_rep, local, 2)  29.7 us
  transfers between devices with their start and end apart: 9, of which 8 were waited for; matrix products, arithmetic and copies ran while one was open for 0% of the time, Pallas kernels for 0%

profile of v1, /device:TPU:1, one launch (start us, length us, event | category | flops | bytes accessed | tf_op | source)
XLA Modules:
  0.0 1330.1 jit_solution(8389657825213751505)
XLA Ops:
  7.2 29.7 %all_gather.15 = s32[2048,2]{0,1:T(2,128)S(1)} all-gather(s32[128,2]{0,1:T(2,128)} %param.7), channel_id=1, replica_groups=mesh['rep'=16,'ep'=32] {'rep'}, dimensions={0}, use_global_device_ids=true | all-gather | bytes 17408 | tf_op jit(solution)/shard_map/all_gather | solution.py:40
  39.3 1.4 fusion
  42.0 1.9 collective-permute-start
  44.0 8.0 collective-permute-done
  52.2 1.9 collective-permute-start.1
  54.1 45.9 %collective-permute-done.1 = bf16[128,4096]{1,0:T(8,128)(2,1)} collective-permute-done((bf16[128,4096]{1,0:T(8,128)(2,1)S(1)}, bf16[128,4096]{1,0:T(8,128)(2,1)}, u32[]{:S(2)}, u32[]{:S(2)}) %collective-permute-start.1) | collective-permute-done | bytes 1048608 | tf_op jit(solution)/shard_map/ppermute | solution.py:17
  100.1 3.1 maximum_select_fusion.2
  103.1 1.9 collective-permute-start.2
  105.1 272.1 %collective-permute-done.2 = bf16[256,4096]{1,0:T(8,128)(2,1)} collective-permute-done((bf16[256,4096]{1,0:T(8,128)(2,1)S(1)}, bf16[256,4096]{1,0:T(8,128)(2,1)}, u32[]{:S(2)}, u32[]{:S(2)}) %collective-permute-start.2) | collective-permute-done | bytes 2097184 | tf_op jit(solution)/shard_map/ppermute | solution.py:17
  377.2 4.7 maximum_select_fusion.1
  381.9 7.8 collective-permute-start.3
  393.0 273.1 %all-reduce = bf16[1024]{0:T(1024)(128)(2,1)S(1)} all-reduce(bf16[1024]{0:T(1024)(128)(2,1)S(1)} %dynamic-update-slice), channel_id=1, replica_groups=mesh['rep'=16,'ep'=32] {'rep'}, use_global_device_ids=true, to_apply=%add | all-reduce | flops 1024 | bytes 4096
  666.1 7.7 fusion.5
  673.8 8.2 multiply_convert_fusion.2
  682.8 70.2 %all-gather.4.cloned.1.call-done = bf16[1792,1024]{1,0:T(8,128)(2,1)} async-done(((bf16[112,1024]{1,0:T(8,128)(2,1)}), bf16[1792,1024]{1,0:T(8,128)(2,1)}) %all-gather.4.cloned.1.call-update) | async-done | bytes 3670032 | tf_op jit(solution)/shard_map/all_gather | solution.py:61
  753.0 6.0 copy.60
  759.0 3.2 fusion.10
  762.2 3.2 fusion.25
  765.5 105.8 %reduce-scatter.3.cloned.1.call-done = f32[64,256]{1,0:T(8,128)} async-done(((f32[2048,256]{1,0:T(8,128)}), f32[64,256]{1,0:T(8,128)}) %reduce-scatter.3.cloned.1.call-update) | async-done | bytes 65552 | tf_op jit(solution)/shard_map/reduce_scatter | solution.py:74
  871.3 1.5 convert_element_type.87
  873.0 61.7 %all-gather.6.cloned.1.call-done = bf16[2048,256]{1,0:T(8,128)(2,1)} async-done(((bf16[64,256]{1,0:T(8,128)(2,1)}), bf16[2048,256]{1,0:T(8,128)(2,1)}) %all-gather.6.cloned.1.call-update) | async-done | bytes 1048592 | tf_op jit(solution)/shard_map/all_gather | solution.py:76
  934.7 1.5 convolution_convert_fusion.2
  936.2 3.8 multiply_reduce_fusion.1
  940.0 103.6 %psum.28 = f32[]{:T(128)} all-reduce(f32[]{:T(128)} %get-tuple-element.8), channel_id=1, replica_groups=mesh['rep'=16,'ep'=32] {'rep','ep'}, use_global_device_ids=true, to_apply=%region_6.7 | all-reduce | flops 1 | bytes 8 | tf_op jit(solution)/shard_map/psum | solution.py:92
  1044.3 3.2 fusion.24
  1047.5 3.2 fusion.26
  1050.8 95.4 %reduce-scatter.5.cloned.1.call-done = f32[64,256]{1,0:T(8,128)} async-done(((f32[2048,256]{1,0:T(8,128)}), f32[64,256]{1,0:T(8,128)}) %reduce-scatter.5.cloned.1.call-update) | async-done | bytes 65552 | tf_op jit(solution)/shard_map/reduce_scatter | solution.py:74
  1146.2 1.5 convert_element_type.90
  1147.7 61.7 %all-gather.8.cloned.1.call-done = bf16[2048,256]{1,0:T(8,128)(2,1)} async-done(((bf16[64,256]{1,0:T(8,128)(2,1)}), bf16[2048,256]{1,0:T(8,128)(2,1)}) %all-gather.8.cloned.1.call-update) | async-done | bytes 1048592 | tf_op jit(solution)/shard_map/all_gather | solution.py:76
  1209.4 1.5 convolution_convert_fusion.1
  1210.9 4.6 fusion.1
  1215.4 103.8 %all-reduce.1 = (f32[]{:T(128)}, f32[]{:T(128)}, f32[]{:T(128)}) all-reduce(f32[]{:T(128)} %get-tuple-element.3, f32[]{:T(128)} %get-tuple-element.2, f32[]{:T(128)} %get-tuple-element.4), channel_id=1, replica_groups=mesh['rep'=16,'ep'=32] {'rep','ep'}, use_global_device_ids=true, to_apply=%region_9.10 | all-reduce | flops 3 | bytes 24 | tf_op jit(solution)/shard_map/psum | solution.py:92
  (59 shorter events, 8.7 us)
Async XLA Ops:
  7.2 34.5 %copy-start = (bf16[128,4096]{1,0:T(8,128)(2,1)S(1)}, bf16[128,4096]{1,0:T(8,128)(2,1)}, u32[]{:S(2)}) copy-start(bf16[128,4096]{1,0:T(8,128)(2,1)} %param.6) | copy-start | bytes 3145732
  7.2 745.8 %all-gather.4.cloned.1.call-start = ((), (), s32[]{:S(2)}) async-start(), calls=%async_computation.2 | async-start | bytes 3899392 | tf_op jit(solution)/shard_map/all_gather | solution.py:61
  40.7 0.8 copy-start.2
  42.0 9.9 collective-permute-start
  52.2 1.9 copy-start.1
  52.2 47.9 %collective-permute-start.1 = (bf16[128,4096]{1,0:T(8,128)(2,1)S(1)}, bf16[128,4096]{1,0:T(8,128)(2,1)}, u32[]{:S(2)}, u32[]{:S(2)}) collective-permute-start(bf16[128,4096]{1,0:T(8,128)(2,1)S(1)} %maximum_select_fusion.9), channel_id=1, source_target_pairs={{0,64},{32,96},{64,0},{96,32},{128,192},{160,224},{192,128},{224,1... | collective-permute-start | bytes 3145736 | tf_op jit(solution)/shard_map/ppermute | solution.py:17
  103.1 274.1 %collective-permute-start.2 = (bf16[256,4096]{1,0:T(8,128)(2,1)S(1)}, bf16[256,4096]{1,0:T(8,128)(2,1)}, u32[]{:S(2)}, u32[]{:S(2)}) collective-permute-start(bf16[256,4096]{1,0:T(8,128)(2,1)S(1)} %maximum_select_fusion.2), channel_id=1, source_target_pairs={{0,128},{32,160},{64,192},{96,224},{128,0},{160,32},{192,64},{224,... | collective-permute-start | bytes 6291464 | tf_op jit(solution)/shard_map/ppermute | solution.py:17
  105.1 284.6 %copy-start.3 = (bf16[128,2]{0,1:T(2,128)(2,1)S(1)}, bf16[128,2]{0,1:T(2,128)(2,1)}, u32[]{:S(2)}) copy-start(bf16[128,2]{0,1:T(2,128)(2,1)} %param.8) | copy-start | bytes 1540
  381.9 284.2 %collective-permute-start.3 = (bf16[512,4096]{1,0:T(8,128)(2,1)}, bf16[512,4096]{1,0:T(8,128)(2,1)}, u32[]{:S(2)}, u32[]{:S(2)}) collective-permute-start(bf16[512,4096]{1,0:T(8,128)(2,1)} %maximum_select_fusion.1), channel_id=1, source_target_pairs={{0,256},{32,288},{64,320},{96,352},{128,384},{160,416},{192,448},{... | collective-permute-start | bytes 12582920 | tf_op jit(solution)/shard_map/ppermute | solution.py:17
  666.1 7.7 copy-start.4
  682.0 189.2 %reduce-scatter.3.cloned.1.call-start = ((), (), s32[]{:S(2)}) async-start(), calls=%async_computation.3 | async-start | bytes 2162688 | tf_op jit(solution)/shard_map/reduce_scatter | solution.py:74
  753.0 6.0 copy-start.5
  765.5 169.2 %all-gather.6.cloned.1.call-start = ((), (), s32[]{:S(2)}) async-start(), calls=%async_computation.4 | async-start | bytes 1081344 | tf_op jit(solution)/shard_map/all_gather | solution.py:76
  872.8 273.4 %reduce-scatter.5.cloned.1.call-start = ((), (), s32[]{:S(2)}) async-start(), calls=%async_computation.5 | async-start | bytes 2162688 | tf_op jit(solution)/shard_map/reduce_scatter | solution.py:74
  940.0 107.5 %copy-start.6 = (f32[1792,256]{1,0:T(8,128)}, f32[1792,256]{1,0:T(8,128)S(1)}, u32[]{:S(2)}) copy-start(f32[1792,256]{1,0:T(8,128)S(1)} %get-tuple-element.9) | copy-start | bytes 5505028
  1050.8 158.6 %all-gather.8.cloned.1.call-start = ((), (), s32[]{:S(2)}) async-start(), calls=%async_computation.6 | async-start | bytes 1081344 | tf_op jit(solution)/shard_map/all_gather | solution.py:76
Sparse Core Ops, SparseCore 0:
  682.2 70.7 all-gather.3
  765.6 105.6 reduce-scatter.2
  875.0 59.6 all-gather.5
  1050.9 95.2 reduce-scatter.4
  1149.7 59.5 all-gather.7
